TPU v7x, 32 devices: a whole 2x2x4 slice. The times are simulated.
32 devices in a mesh: groups: 2 (over x), rows: 16 (over z, y, core).
Axes of the slice: x: 2, y: 2, z: 4, core: 2. Of those that a mesh axis runs over, the one named last changes fastest.
Arguments:
- image_query: bfloat16 [12288, 2048], P(('groups', 'rows')), parts along dimension 0, may hold values from -40 to 40
- image_pairs: bfloat16 [2, 12288, 2048], P(None, ('groups', 'rows')), parts along dimension 1, may hold values from -6 to 6
- text_query: bfloat16 [512, 2048], P(('groups', 'rows')), parts along dimension 0, may hold values from -40 to 40
- text_pairs: bfloat16 [2, 512, 2048], P(None, ('groups', 'rows')), parts along dimension 1, may hold values from -6 to 6
- text_mask: int32 [512], P('groups'), parts along dimension 0, may hold values 0 or 1
- window_offsets: int32 [16, 2], replicated, may hold values from -1 to 1, as said below
- timestep: int32 [1], replicated, may hold values from 0 to 49
- gate_table: float32 [50, 2, 2048], replicated, may hold values from 0.5 to 2
Outputs:
- image_out: bfloat16 [12288, 2048], P(('groups', 'rows')), parts along dimension 0
- text_out: bfloat16 [512, 2048], P(('groups', 'rows')), parts along dimension 0
There are 2 independent parts, one for each index of `groups`. A program takes and returns all parts, laid end to end along the dimension named above; an argument that names none is the same for every part. Nothing has to cross between parts.
Inputs may be any that keep to these rules, and one draw needn't show every extreme that they name: window_offsets[h, 0] is -1 or 0 and window_offsets[h, 1] is 0 or 1; some head has -1 and some head has 1.
All inputs are finite; a program needn't handle non-finite values.
Results may differ from a plain program's by a relative error of at most 0.02.
Values may be sent and summed in bfloat16 or wider, within the bound.
A program may use at most 128 MiB of HBM per device.

v0:
```python
import math
import jax
import jax.numpy as jnp
from jax import lax
from jax.sharding import PartitionSpec as P

TILE = 384
masked_score = -1e30


def extended_2(cells, sides, width):
    for axis, dim in sides:
        count = lax.axis_size(axis)
        ends = count - 1
        head = lax.slice_in_dim(cells, 0, width, axis=dim)
        tail = lax.slice_in_dim(cells, cells.shape[dim] - width, cells.shape[dim], axis=dim)
        cells = jnp.concatenate(
            [
                lax.ppermute(tail, axis, [(i, (i + 1) % count) for i in range(ends)]),
                cells,
                lax.ppermute(head, axis, [((i + 1) % count, i) for i in range(ends)]),
            ],
            axis=dim,
        )
    return cells


def attend_tiles(queries, key_rows, value_rows, allowed, scaling):
    scores = (
        jnp.einsum("tqhe,tkhe->tqhk", queries, key_rows, preferred_element_type=jnp.float32)
        * scaling
    )
    scores = jnp.where(allowed, scores, masked_score)
    maxima = jnp.max(scores, axis=-1)
    exponent = jnp.where(allowed, jnp.exp(scores - maxima[..., None]), 0.0)
    totals = jnp.sum(exponent, axis=-1)
    summed = jnp.einsum(
        "tqhk,tkhe->tqhe",
        exponent.astype(jnp.bfloat16),
        value_rows,
        preferred_element_type=jnp.float32,
    )
    return (maxima, totals, summed.astype(jnp.bfloat16))


def attend_rows(queries, key_rows, value_rows, allowed, scaling):
    scores = (
        jnp.einsum("qhe,khe->qhk", queries, key_rows, preferred_element_type=jnp.float32) * scaling
    )
    scores = jnp.where(allowed, scores, masked_score)
    maxima = jnp.max(scores, axis=-1)
    exponent = jnp.where(allowed, jnp.exp(scores - maxima[..., None]), 0.0)
    totals = jnp.sum(exponent, axis=-1)
    summed = jnp.einsum(
        "qhk,khe->qhe",
        exponent.astype(jnp.bfloat16),
        value_rows,
        preferred_element_type=jnp.float32,
    )
    return (maxima, totals, summed.astype(jnp.bfloat16))


def combine_groups(groups):
    largest = groups[0][0]
    for member in groups[1:]:
        largest = jnp.maximum(largest, member[0])
    totals = 0.0
    summed = 0.0
    for member in groups:
        factor = jnp.exp(member[0] - largest)
        totals = totals + member[1] * factor
        summed = summed + member[2].astype(jnp.float32) * factor[..., None]
    return summed / totals[..., None]


def on_device(
    image_query,
    image_pairs,
    text_query,
    text_pairs,
    text_mask,
    window_offsets,
    timestep,
    gate_table,
):
    rows_dev, width = image_query.shape
    tiles_dev = rows_dev // TILE
    head_count = window_offsets.shape[0]
    head_width = width // head_count
    scaling = 1.0 / math.sqrt(head_width)
    position = lax.axis_index("rows")
    tiles_all = tiles_dev * lax.axis_size("rows")
    first_tile = position * tiles_dev
    reach_back = window_offsets[:, 0]
    reach_ahead = window_offsets[:, 1]
    text_queries, text_gathered = (
        lax.all_gather(text_query, "rows", axis=0, tiled=True),
        lax.all_gather(text_pairs, "rows", axis=1, tiled=True),
    )
    text_keys = text_gathered[0].reshape(-1, head_count, head_width)
    text_values = text_gathered[1].reshape(-1, head_count, head_width)
    text_allowed = (text_mask == 1)[None, None, :]
    queries = image_query.reshape(tiles_dev, TILE, head_count, head_width)
    local_keys = image_pairs[0].reshape(tiles_dev, TILE, head_count, head_width)
    local_values = image_pairs[1].reshape(tiles_dev, TILE, head_count, head_width)

    def permitted(offset):
        target = first_tile + jnp.arange(tiles_dev, dtype=jnp.int32) + offset
        inside = (target >= 0) & (target < tiles_all)
        within = (reach_back <= offset) & (offset <= reach_ahead)
        return (inside[:, None] & within[None, :])[:, None, :, None]

    flat_queries = image_query.reshape(rows_dev, head_count, head_width)
    text_group = attend_rows(flat_queries, text_keys, text_values, text_allowed, scaling)
    text_group = (
        text_group[0].reshape(tiles_dev, TILE, head_count),
        text_group[1].reshape(tiles_dev, TILE, head_count),
        text_group[2].reshape(tiles_dev, TILE, head_count, head_width),
    )
    groups = [attend_tiles(queries, local_keys, local_values, permitted(0), scaling), text_group]
    extended = extended_2(image_pairs, (("rows", 1),), TILE)
    extended = extended.reshape(2, tiles_dev + 2, TILE, head_count, head_width)
    for offset in (-1, 1):
        groups.append(
            attend_tiles(
                queries,
                extended[0, 1 + offset : 1 + offset + tiles_dev],
                extended[1, 1 + offset : 1 + offset + tiles_dev],
                permitted(offset),
                scaling,
            )
        )
    gate_rows = lax.dynamic_index_in_dim(gate_table, timestep[0], 0, keepdims=False)
    attended = combine_groups(groups).reshape(rows_dev, width)
    image_out = (attended * gate_rows[0]).astype(jnp.bfloat16)
    text_flat = text_queries.reshape(-1, head_count, head_width)
    image_keys = image_pairs[0].reshape(rows_dev, head_count, head_width)
    image_values = image_pairs[1].reshape(rows_dev, head_count, head_width)
    every_key = jnp.ones((1, 1, rows_dev), dtype=bool)
    maxima, totals, summed = attend_rows(text_flat, image_keys, image_values, every_key, scaling)
    text_dev = text_query.shape[0]
    text_start = position * text_dev
    global_max = lax.pmax(maxima, "rows")
    factor = jnp.exp(maxima - global_max)
    scaled_summed = summed.astype(jnp.float32) * factor[..., None]
    scaled_totals = totals * factor
    whole_summed, whole_totals = lax.psum((scaled_summed, scaled_totals), "rows")
    shared_summed = lax.dynamic_slice_in_dim(whole_summed, text_start, text_dev, 0)
    shared_totals = lax.dynamic_slice_in_dim(whole_totals, text_start, text_dev, 0)
    remote = (
        lax.dynamic_slice_in_dim(global_max, text_start, text_dev, 0),
        shared_totals,
        shared_summed,
    )
    own_rows = text_query.reshape(text_dev, head_count, head_width)
    own_text = attend_rows(own_rows, text_keys, text_values, text_allowed, scaling)
    text_attended = combine_groups([remote, own_text]).reshape(text_dev, width)
    text_out = (text_attended * gate_rows[1]).astype(jnp.bfloat16)
    return (image_out, text_out)


def solution(mesh):
    placed = (
        P(("groups", "rows"), None),
        P(None, ("groups", "rows"), None),
        P(("groups", "rows"), None),
        P(None, ("groups", "rows"), None),
        P("groups"),
        P(),
        P(),
        P(),
    )
    return jax.shard_map(
        on_device,
        mesh=mesh,
        in_specs=placed,
        out_specs=(P(("groups", "rows"), None), P(("groups", "rows"), None)),
        check_vma=False,
    )
```

profile of v0, /device:TPU:0, one launch (start us, length us, event | category | flops | bytes accessed | tf_op | source)
XLA Modules:
  0.0 297.9 jit_solution(4161448792035331032)
XLA Ops:
  8.0 4.0 %collective-permute-start = (bf16[2,384,2048]{2,1,0:T(8,128)(2,1)}, bf16[2,384,2048]{2,1,0:T(8,128)(2,1)}, u32[]{:S(2)}, u32[]{:S(2)}) collective-permute-start(bf16[2,384,2048]{2,1,0:T(8,128)(2,1)} %param.9), channel_id=1, source_target_pairs={{0,1},{1,2},{2,3},{3,4},{4,5},{5,6},{6,7},{7,8},{8,9},{9,10},{10,1... | collective-permute-start | bytes 9437192 | tf_op jit(solution)/shard_map/ppermute | solution.py:19
  17.3 4.1 %fusion.134 = (bf16[1,384,2048]{2,1,0:T(8,128)(2,1)}, bf16[1,384,2048]{2,1,0:T(8,128)(2,1)}) fusion(bf16[2,384,2048]{2,1,0:T(8,128)(2,1)} %param.9), kind=kLoop, calls=%fused_computation.155 | loop fusion | bytes 6291456 | tf_op jit(solution)/shard_map/slice | solution.py:104
  28.3 3.6 %copy-done.2 = f32[16,384,384]{2,1,0:T(8,128)} copy-done((f32[16,384,384]{2,1,0:T(8,128)}, f32[16,384,384]{2,1,0:T(8,128)S(1)}, u32[]{:S(2)}) %copy-start.2) | copy-done | bytes 9437208
  31.9 3.5 %fusion.67 = bf16[16,384,128]{1,2,0:T(8,128)(2,1)} fusion(bf16[384,16,128]{0,2,1:T(8,128)(2,1)S(1)} %bitcast.291, f32[16,384,384]{2,1,0:T(8,128)S(1)} %get-tuple-element.26, f32[384,16]{0,1:T(8,128)S(1)} %get-tuple-element.25, pred[16]{0:T(512)(128)(4,1)S(1)} %get-tuple-element.24), kind=kOutput, calls=%fused_computation.81 | convolution fusion | flops 616562688 | bytes 12607504 | tf_op jit(solution)/shard_map/tqhk,tkhe->tqhe/dot_general | solution.py:37
  35.5 28.8 %all-gather.5.cloned.1.call-done = bf16[256,2048]{1,0:T(8,128)(2,1)} async-done(((bf16[16,2048]{1,0:T(8,128)(2,1)}), bf16[256,2048]{1,0:T(8,128)(2,1)}) %all-gather.5.cloned.1.call-update) | async-done | bytes 1048592 | tf_op jit(solution)/shard_map/all_gather | solution.py:97
  66.7 4.9 %bitcast_reduce_fusion.3 = (f32[256,16]{0,1:T(8,128)S(1)}, f32[16,384,256]{2,1,0:T(8,128)}) fusion(bf16[384,16,128]{0,2,1:T(8,128)(2,1)S(1)} %bitcast.287, bf16[256,16,128]{0,2,1:T(8,128)(2,1)} %bitcast.294), kind=kOutput, calls=%fused_computation.23 | convolution fusion | flops 405794816 | bytes 8929280 | tf_op jit(solution)/shard_map/qhe,khe->qhk/dot_general | solution.py:48
  71.6 66.7 %pmax.7 = f32[256,16]{0,1:T(8,128)S(1)} all-reduce(f32[256,16]{0,1:T(8,128)S(1)} %get-tuple-element.35), channel_id=1, replica_groups=mesh['groups'=2,'rows'=16] {'rows'}, use_global_device_ids=true, to_apply=%region_9.10 | all-reduce | flops 4096 | bytes 32768 | tf_op jit(solution)/shard_map/pmax | solution.py:143
  138.3 4.0 %fusion.15 = f32[256,16]{0,1:T(8,128)S(1)} fusion(f32[16,384,256]{2,1,0:T(8,128)} %get-tuple-element.36, f32[256,16]{0,1:T(8,128)S(1)} %get-tuple-element.35), kind=kLoop, calls=%fused_computation.30 | loop fusion | flops 4714496 | bytes 6324224 | tf_op jit(solution)/shard_map/reduce_sum | solution.py:53
  142.9 4.4 %bitcast_multiply_fusion.2 = f32[256,16,128]{2,0,1:T(8,128)} fusion(bf16[384,16,128]{0,2,1:T(8,128)(2,1)} %bitcast.290, f32[16,384,256]{2,1,0:T(8,128)S(1)} %copy-done.1, f32[256,16]{0,1:T(8,128)S(1)} %get-tuple-element.35, f32[256,16]{0,1:T(8,128)S(1)} %get-tuple-element.6), kind=kOutput, calls=%fused_computation.79 | convolution fusion | flops 408944640 | bytes 9994240 | tf_op jit(solution)/shard_map/qhk,khe->qhe/dot_general | solution.py:54
  147.3 58.2 %psum.15 = f32[256,16]{0,1:T(8,128)S(1)} all-reduce(f32[256,16]{0,1:T(8,128)S(1)} %get-tuple-element.5), channel_id=1, replica_groups=mesh['groups'=2,'rows'=16] {'rows'}, use_global_device_ids=true, to_apply=%region_13.14 | all-reduce | flops 4096 | bytes 32768 | tf_op jit(solution)/shard_map/psum | solution.py:147
  205.5 7.6 %pad_maximum_fusion = bf16[2,1152,2048]{2,1,0:T(8,128)(2,1)} fusion(bf16[2,384,2048]{2,1,0:T(8,128)(2,1)} %collective-permute-done.1, bf16[2,384,2048]{2,1,0:T(8,128)(2,1)} %param.9, bf16[2,384,2048]{2,1,0:T(8,128)(2,1)} %collective-permute-done), kind=kLoop, calls=%fused_computation | loop fusion | flops 28311552 | bytes 18874368 | tf_op jit(solution)/shard_map/concatenate | solution.py:17
  213.1 11.0 %copy.104 = bf16[288,8,16,128]{3,2,1,0:T(8,128)(2,1)} copy(bf16[288,8,16,128]{3,1,2,0:T(8,128)(2,1)} %bitcast.284) | data formatting | bytes 18874368
  224.2 5.6 %fusion.133 = (bf16[1,1,384,16,128]{4,3,2,1,0:T(8,128)(2,1)}, bf16[1,1,384,16,128]{4,3,2,1,0:T(8,128)(2,1)}, bf16[1,1,384,16,128]{4,3,2,1,0:T(8,128)(2,1)}, bf16[1,1,384,16,128]{4,3,2,1,0:T(8,128)(2,1)S(1)}) fusion(bf16[2,3,384,16,128]{4,3,2,1,0:T(8,128)(2,1)} %bitcast.285), kind=kLoop, calls=%fused_computation.154 | loop fusion | bytes 12582912 | tf_op jit(solution)/shard_map/slice | solution.py:128
  229.8 2.8 copy.99
  234.6 3.3 %bitcast_reduce_fusion = (f32[384,16]{0,1:T(8,128)S(1)}, f32[16,384,384]{2,1,0:T(8,128)S(1)}) fusion(pred[16]{0:T(512)(128)(4,1)S(1)} %get-tuple-element.23, bf16[1,1,384,16,128]{4,3,2,1,0:T(8,128)(2,1)} %get-tuple-element.13, bf16[384,2048]{1,0:T(8,128)(2,1)S(1)} %copy-done), kind=kOutput, calls=%fused_computation.2 | convolution fusion | flops 611051520 | bytes 12607504 | tf_op jit(solution)/shard_map/tqhe,tkhe->tqhk/dot_general | solution.py:30
  240.6 3.5 %fusion.73 = bf16[16,128,384]{2,1,0:T(8,128)(2,1)} fusion(f32[16,384,384]{2,1,0:T(8,128)S(1)} %get-tuple-element.28, f32[384,16]{0,1:T(8,128)S(1)} %get-tuple-element.27, pred[16]{0:T(512)(128)(4,1)S(1)} %get-tuple-element.23, bf16[1,1,384,16,128]{2,4,3,1,0:T(8,128)(2,1)S(1)} %copy-done.7), kind=kOutput, calls=%fused_computation.83 | convolution fusion | flops 616562688 | bytes 12607504 | tf_op jit(solution)/shard_map/tqhk,tkhe->tqhe/dot_general | solution.py:37
  246.3 5.5 %fusion.6 = (f32[384,16]{0,1:T(8,128)S(1)}, f32[384,16]{0,1:T(8,128)S(1)}) fusion(f32[16,384,384]{2,1,0:T(8,128)S(1)} %bitcast.283, f32[384,16]{0,1:T(8,128)S(1)} %get-tuple-element.25, pred[16]{0:T(512)(128)(4,1)S(1)} %get-tuple-element.24, f32[384,16]{0,1:T(8,128)S(1)} %get-tuple-element.29, f32[16,384,384]{2,1,0:T(8,128)S(1)} %get-tuple-element.30, ...), kind=kLoop, calls=%fused_computation.16 | loop fusion | flops 23580672 | bytes 18972704 | tf_op jit(solution)/shard_map/reduce_sum | solution.py:36
  251.8 3.5 %fusion.70 = bf16[16,128,384]{2,1,0:T(8,128)(2,1)} fusion(f32[16,384,384]{2,1,0:T(8,128)S(1)} %get-tuple-element.30, f32[384,16]{0,1:T(8,128)S(1)} %get-tuple-element.29, pred[16]{0:T(512)(128)(4,1)S(1)} %get-tuple-element.22, bf16[1,1,384,16,128]{2,4,3,1,0:T(8,128)(2,1)S(1)} %copy-done.6), kind=kOutput, calls=%fused_computation.82 | convolution fusion | flops 616562688 | bytes 12607504 | tf_op jit(solution)/shard_map/tqhk,tkhe->tqhe/dot_general | solution.py:37
  255.4 6.8 %fusion.135 = (bf16[1,256,2048]{2,0,1:T(2,128)(2,1)}, bf16[1,256,2048]{2,0,1:T(2,128)(2,1)}) fusion(bf16[2,256,2048]{2,0,1:T(2,128)(2,1)} %all-gather.3.cloned.1.call-done), kind=kLoop, calls=%fused_computation.156 | loop fusion | bytes 4194304 | tf_op jit(solution)/shard_map/slice | solution.py:101
  262.2 5.8 %copy.67 = bf16[1,256,2048]{1,2,0:T(8,128)(2,1)} copy(bf16[1,256,2048]{2,0,1:T(2,128)(2,1)} %get-tuple-element.18) | data formatting | bytes 2097152 | tf_op jit(solution)/shard_map/slice | solution.py:101
  268.0 4.8 %copy.96 = bf16[1,256,2048]{1,2,0:T(8,128)(2,1)S(1)} copy(bf16[1,256,2048]{2,0,1:T(2,128)(2,1)} %get-tuple-element.19) | data formatting | bytes 2097152
  276.9 4.5 %fusion.52 = f32[1,384,16,128]{1,3,2,0:T(8,128)} fusion(bf16[16,384,128]{1,2,0:T(8,128)(2,1)S(1)} %copy-done.10, bf16[16,128,384]{2,1,0:T(8,128)(2,1)S(1)} %copy-done.11, bf16[16,128,384]{2,1,0:T(8,128)(2,1)S(1)} %copy-done.12, f32[384,16]{0,1:T(8,128)S(1)} %get-tuple-element.7, f32[384,16]{0,1:T(8,128)S(1)} %get-tuple-element.11, ...), kind=kOutput, calls=%fused_computation.63 | convolution fusion | flops 420741120 | bytes 15352064 | tf_op jit(solution)/shard_map/qhk,khe->qhe/dot_general | solution.py:54
  281.4 3.6 %copy.73 = f32[384,2048]{1,0:T(8,128)} copy(f32[384,2048]{0,1:T(8,128)} %bitcast.295) | data formatting | bytes 6291456 | tf_op jit(solution)/shard_map/reshape | solution.py:134
  288.0 3.4 %multiply_convert_fusion = bf16[384,2048]{1,0:T(8,128)(2,1)} fusion(f32[384,2048]{1,0:T(8,128)} %copy.73, f32[2048]{0:T(1024)S(1)} %bitcast.296), kind=kLoop, calls=%fused_computation.72 | loop fusion | flops 1572864 | bytes 4726784 | tf_op jit(solution)/shard_map/convert_element_type | solution.py:135
  (63 shorter events, 29.2 us)
Async XLA Ops:
  7.2 18.7 %copy-start = (bf16[384,2048]{1,0:T(8,128)(2,1)S(1)}, bf16[384,2048]{1,0:T(8,128)(2,1)}, u32[]{:S(2)}) copy-start(bf16[384,2048]{1,0:T(8,128)(2,1)} %param.8) | copy-start | bytes 4718596
  7.2 57.1 %all-gather.5.cloned.1.call-start = ((), (), s32[]{:S(2)}) async-start(), calls=%async_computation.1 | async-start | bytes 1114112 | tf_op jit(solution)/shard_map/all_gather | solution.py:97
  7.9 247.5 %all-gather.3.cloned.1.call-start = ((), (), s32[]{:S(2)}) async-start(), calls=%async_computation | async-start | bytes 2228224 | tf_op jit(solution)/shard_map/all_gather | solution.py:98
  8.0 197.5 %collective-permute-start = (bf16[2,384,2048]{2,1,0:T(8,128)(2,1)}, bf16[2,384,2048]{2,1,0:T(8,128)(2,1)}, u32[]{:S(2)}, u32[]{:S(2)}) collective-permute-start(bf16[2,384,2048]{2,1,0:T(8,128)(2,1)} %param.9), channel_id=1, source_target_pairs={{0,1},{1,2},{2,3},{3,4},{4,5},{5,6},{6,7},{7,8},{8,9},{9,10},{10,1... | collective-permute-start | bytes 9437192 | tf_op jit(solution)/shard_map/ppermute | solution.py:19
  12.0 193.5 %collective-permute-start.1 = (bf16[2,384,2048]{2,1,0:T(8,128)(2,1)}, bf16[2,384,2048]{2,1,0:T(8,128)(2,1)}, u32[]{:S(2)}, u32[]{:S(2)}) collective-permute-start(bf16[2,384,2048]{2,1,0:T(8,128)(2,1)} %param.9), channel_id=1, source_target_pairs={{1,0},{2,1},{3,2},{4,3},{5,4},{6,5},{7,6},{8,7},{9,8},{10,9},{11,1... | collective-permute-start | bytes 9437192 | tf_op jit(solution)/shard_map/ppermute | solution.py:21
  15.0 270.7 %all-reduce.2.cloned.1.call-start = ((), (), s32[]{:S(2)}) async-start(), calls=%async_computation.2 | async-start | bytes 4194304 | tf_op jit(solution)/shard_map/psum | solution.py:147
  17.3 4.1 %copy-start.9 = (s32[256]{0:T(256)S(1)}, s32[256]{0:T(256)}, u32[]{:S(2)}) copy-start(s32[256]{0:T(256)} %param.12) | copy-start | bytes 3076
  25.8 6.1 %copy-start.3 = (bf16[1,384,2048]{1,2,0:T(8,128)(2,1)S(1)}, bf16[1,384,2048]{1,2,0:T(8,128)(2,1)}, u32[]{:S(2)}) copy-start(bf16[1,384,2048]{1,2,0:T(8,128)(2,1)} %copy.57) | copy-start | bytes 4718596
  28.3 3.6 %copy-start.2 = (f32[16,384,384]{2,1,0:T(8,128)}, f32[16,384,384]{2,1,0:T(8,128)S(1)}, u32[]{:S(2)}) copy-start(f32[16,384,384]{2,1,0:T(8,128)S(1)} %get-tuple-element.26) | copy-start | bytes 28311556
  138.3 4.6 %copy-start.1 = (f32[16,384,256]{2,1,0:T(8,128)S(1)}, f32[16,384,256]{2,1,0:T(8,128)}, u32[]{:S(2)}) copy-start(f32[16,384,256]{2,1,0:T(8,128)} %get-tuple-element.36) | copy-start | bytes 18874372
  237.9 2.7 copy-start.7
  240.6 3.5 %copy-start.5 = (bf16[1,1,384,16,128]{4,3,2,1,0:T(8,128)(2,1)S(1)}, bf16[1,1,384,16,128]{4,3,2,1,0:T(8,128)(2,1)}, u32[]{:S(2)}) copy-start(bf16[1,1,384,16,128]{4,3,2,1,0:T(8,128)(2,1)} %get-tuple-element.14) | copy-start | bytes 4718596
  240.6 5.4 %slice-start = ((s8[9437184]{0:T(1024)(128)(4,1)}), s8[4194304]{0:T(1024)(128)(4,1)S(1)}, s32[]{:S(2)}) async-start(s8[9437184]{0:T(1024)(128)(4,1)} %bitcast.282), calls=%async_computation.3 | async-start | bytes 8388608
  240.6 5.4 %slice-start.1 = ((s8[9437184]{0:T(1024)(128)(4,1)}), s8[1048576]{0:T(1024)(128)(4,1)S(1)}, s32[]{:S(2)}) async-start(s8[9437184]{0:T(1024)(128)(4,1)} %bitcast.282), calls=%async_computation.4 | async-start | bytes 2097152
  244.1 2.2 slice-start.2
  246.3 5.5 %copy-start.6 = (bf16[1,1,384,16,128]{2,4,3,1,0:T(8,128)(2,1)S(1)}, bf16[1,1,384,16,128]{2,4,3,1,0:T(8,128)(2,1)}, u32[]{:S(2)}) copy-start(bf16[1,1,384,16,128]{2,4,3,1,0:T(8,128)(2,1)} %copy.99) | copy-start | bytes 4718596
  274.2 1.8 copy-start.4
  274.2 1.8 copy-start.10
  274.2 2.2 copy-start.11
  274.2 2.7 copy-start.12
  281.4 3.6 %copy-start.8 = (bf16[16,2048]{1,0:T(8,128)(2,1)S(1)}, bf16[16,2048]{1,0:T(8,128)(2,1)}, u32[]{:S(2)}) copy-start(bf16[16,2048]{1,0:T(8,128)(2,1)} %param.10) | copy-start | bytes 196612
Sparse Core Ops, SparseCore 0:
  10.2 54.0 all-gather.4
  66.5 43.8 all-gather.2
  147.5 95.1 all-reduce.1
where the time goes:
time: 299 us; the launch traced here: 298 us
  blocking collectives  125 us (42%)
  local copies, waits for them, and re-layouts  61.2 us (20%)
  matrix products  35.5 us (12%)
  waiting for transfers between devices  29.6 us (10%)
  other arithmetic  26.6 us (9%)
  between operations  14.7 us (5%)
  starting transfers between devices  5.42 us (2%)
    pmax x1, blocking collectives, on_device(): global_max = lax.pmax(maxima, 'rows')  66.7 us
    psum x1, blocking collectives, on_device(): lax.psum((scaled_summed, scaled_totals), 'rows')  58.2 us
    unnamed x38, local copies, waits for them, and re-layouts  29.6 us
    all_gather x1, waiting for transfers between devices, on_device(): lax.all_gather(text_query, 'rows', axis=0, tiled=True)  28.8 us
    slice x2, local copies, waits for them, and re-layouts, on_device(): text_values = text_gathered[1].reshape(-1, head_count, head_width)  12.6 us
    dot_general x3, matrix products, attend_tiles(): jnp.einsum('tqhk,tkhe->tqhe', exponent.astype(jnp.bfloat16), value_rows,...  10.6 us
    dot_general x3, matrix products, attend_rows(): jnp.einsum('qhk,khe->qhe', exponent.astype(jnp.bfloat16), value_rows, pre...  10.5 us
    reduce_sum x2, other arithmetic, attend_tiles(): totals = jnp.sum(exponent, axis=-1)  8.14 us
  transfers between devices with their start and end apart: 5, of which 1 were waited for; matrix products, arithmetic and copies ran while one was open for 38% of the time, Pallas kernels for 0%

commit v1 on v0

--- a/solution.py
+++ b/solution.py
@@ -6,6 +6,27 @@
 
 TILE = 384
 masked_score = -1e30
+
+
+def collect(x, axis, dim):
+    size, position, width = (lax.axis_size(axis), lax.axis_index(axis), x.shape[dim])
+    right = [(i, (i + 1) % size) for i in range(size)]
+    left = [(i, (i - 1) % size) for i in range(size)]
+    out = jnp.zeros((*x.shape[:dim], size * width, *x.shape[dim + 1 :]), x.dtype)
+    out = lax.dynamic_update_slice_in_dim(out, x, position * width, axis=dim)
+    from_left = from_right = x
+    halfway = size // 2
+    for turn in range(1, halfway + 1):
+        from_left = lax.ppermute(from_left, axis, right)
+        out = lax.dynamic_update_slice_in_dim(
+            out, from_left, (position - turn) % size * width, axis=dim
+        )
+        if turn < size - halfway:
+            from_right = lax.ppermute(from_right, axis, left)
+            out = lax.dynamic_update_slice_in_dim(
+                out, from_right, (position + turn) % size * width, axis=dim
+            )
+    return out
 
 
 def extended_2(cells, sides, width):
@@ -94,7 +115,7 @@
     reach_back = window_offsets[:, 0]
     reach_ahead = window_offsets[:, 1]
     text_queries, text_gathered = (
-        lax.all_gather(text_query, "rows", axis=0, tiled=True),
+        collect(text_query, "rows", 0),
         lax.all_gather(text_pairs, "rows", axis=1, tiled=True),
     )
     text_keys = text_gathered[0].reshape(-1, head_count, head_width)

time: 299 us -> 514 us (1.72); the launches traced: 298 us -> 505 us
  starting transfers between devices: 5.42 us -> 126 us
  local copies, waits for them, and re-layouts: 61.2 us -> 159 us
  waiting for transfers between devices: 29.6 us -> 17.6 us
  matrix products: 35.5 us -> 42.9 us
  blocking collectives: 125 us -> 119 us
    ppermute x0 -> x15, starting transfers between devices: none -> 119 us  [the longest x8 86.1 us: collect(): from_left = lax.ppermute(from_left, axis, right)]
    dynamic_update_slice x0 -> x16, local copies, waits for them, and re-layouts: none -> 101 us  [the longest x8 48.1 us: collect(): lax.dynamic_update_slice_in_dim(out, from_left, (position - turn) % size...]
    all_gather x1 -> x0, waiting for transfers between devices: 28.8 us -> none  [on_device(): lax.all_gather(text_query, 'rows', axis=0, tiled=True)]
    ppermute x0 -> x15, waiting for transfers between devices: none -> 17.5 us  [the longest x8 11.3 us: collect(): from_left = lax.ppermute(from_left, axis, right)]
    pmax x1, blocking collectives: 66.7 us -> 60 us  [on_device(): global_max = lax.pmax(maxima, 'rows')]
    unnamed x38 -> x43, local copies, waits for them, and re-layouts: 29.6 us -> 27.1 us
  transfers between devices with their start and end apart: 5 -> 19, of which waited for: 1 -> 5; matrix products, arithmetic and copies ran while one was open for 38% -> 43% of each run, Pallas kernels for 0% -> 0%
where the time goes in v1:
time: 514 us; the launch traced here: 505 us
  local copies, waits for them, and re-layouts  159 us (31%)
  starting transfers between devices  126 us (25%)
  blocking collectives  119 us (23%)
  matrix products  42.9 us (8%)
  other arithmetic  25.9 us (5%)
  waiting for transfers between devices  17.6 us (3%)
  between operations  15.3 us (3%)
    ppermute x8, starting transfers between devices, collect(): from_left = lax.ppermute(from_left, axis, right)  86.1 us
    pmax x1, blocking collectives, on_device(): global_max = lax.pmax(maxima, 'rows')  60 us
    psum x1, blocking collectives, on_device(): lax.psum((scaled_summed, scaled_totals), 'rows')  58.8 us
    dynamic_update_slice x8, local copies, waits for them, and re-layouts, collect(): lax.dynamic_update_slice_in_dim(out, from_left, (position - turn) % size...  48.1 us
    dynamic_update_slice x7, local copies, waits for them, and re-layouts, collect(): lax.dynamic_update_slice_in_dim(out, from_right, (position + turn) % size...  47.4 us
    ppermute x7, starting transfers between devices, collect(): from_right = lax.ppermute(from_right, axis, left)  32.6 us
    unnamed x43, local copies, waits for them, and re-layouts  27.1 us
    dot_general x3, matrix products, attend_tiles(): jnp.einsum('tqhk,tkhe->tqhe', exponent.astype(jnp.bfloat16), value_rows,...  14.9 us
  transfers between devices with their start and end apart: 19, of which 5 were waited for; matrix products, arithmetic and copies ran while one was open for 43% of the time, Pallas kernels for 0%

profile of v1, /device:TPU:0, one launch (start us, length us, event | category | flops | bytes accessed | tf_op | source)
XLA Modules:
  0.0 505.3 jit_solution(1659386276427971232)
XLA Ops:
  14.0 6.9 %collective-permute-done.2 = bf16[16,2048]{0,1:T(8,128)(2,1)S(1)} collective-permute-done((bf16[16,2048]{0,1:T(8,128)(2,1)S(1)}, bf16[16,2048]{0,1:T(8,128)(2,1)S(1)}, u32[]{:S(2)}, u32[]{:S(2)}) %collective-permute-start.2) | collective-permute-done | bytes 65568 | tf_op jit(solution)/shard_map/ppermute | solution.py:20
  44.3 17.0 %collective-permute-start.7 = (bf16[16,2048]{0,1:T(8,128)(2,1)}, bf16[16,2048]{0,1:T(8,128)(2,1)}, u32[]{:S(2)}, u32[]{:S(2)}) collective-permute-start(bf16[16,2048]{0,1:T(8,128)(2,1)} %collective-permute-done.5), channel_id=1, source_target_pairs={{0,15},{1,0},{2,1},{3,2},{4,3},{5,4},{6,5},{7,6},{8,7},{9,8},{10,9... | collective-permute-start | bytes 196616 | tf_op jit(solution)/shard_map/ppermute | solution.py:25
  64.8 58.5 %collective-permute-start.8 = (bf16[16,2048]{0,1:T(8,128)(2,1)}, bf16[16,2048]{0,1:T(8,128)(2,1)}, u32[]{:S(2)}, u32[]{:S(2)}) collective-permute-start(bf16[16,2048]{0,1:T(8,128)(2,1)} %collective-permute-done.6), channel_id=1, source_target_pairs={{0,1},{1,2},{2,3},{3,4},{4,5},{5,6},{6,7},{7,8},{8,9},{9,10},{10,1... | collective-permute-start | bytes 196616 | tf_op jit(solution)/shard_map/ppermute | solution.py:20
  126.3 11.6 %collective-permute-start.10 = (bf16[16,2048]{0,1:T(8,128)(2,1)}, bf16[16,2048]{0,1:T(8,128)(2,1)}, u32[]{:S(2)}, u32[]{:S(2)}) collective-permute-start(bf16[16,2048]{0,1:T(8,128)(2,1)} %collective-permute-done.8), channel_id=1, source_target_pairs={{0,1},{1,2},{2,3},{3,4},{4,5},{5,6},{6,7},{7,8},{8,9},{9,10},{10,1... | collective-permute-start | bytes 196616 | tf_op jit(solution)/shard_map/ppermute | solution.py:20
  149.0 7.7 %fusion.67 = bf16[16,384,128]{1,2,0:T(8,128)(2,1)} fusion(bf16[384,16,128]{0,2,1:T(8,128)(2,1)} %bitcast.290, f32[16,384,384]{2,1,0:T(8,128)} %get-tuple-element.26, f32[384,16]{0,1:T(8,128)S(1)} %get-tuple-element.25, pred[16]{0:T(512)(128)(4,1)S(1)} %get-tuple-element.24), kind=kOutput, calls=%fused_computation.81 | convolution fusion | flops 616562688 | bytes 12607504 | tf_op jit(solution)/shard_map/tqhk,tkhe->tqhe/dot_general | solution.py:58
  171.2 6.4 %collective-permute-start.16 = (bf16[16,2048]{0,1:T(8,128)(2,1)}, bf16[16,2048]{0,1:T(8,128)(2,1)}, u32[]{:S(2)}, u32[]{:S(2)}) collective-permute-start(bf16[16,2048]{0,1:T(8,128)(2,1)} %collective-permute-done.14), channel_id=1, source_target_pairs={{0,1},{1,2},{2,3},{3,4},{4,5},{5,6},{6,7},{7,8},{8,9},{9,10},{10,1... | collective-permute-start | bytes 196616 | tf_op jit(solution)/shard_map/ppermute | solution.py:20
  184.6 6.1 %dynamic_update_slice.49 = bf16[256,2048]{0,1:T(8,128)(2,1)} dynamic-update-slice(bf16[256,2048]{0,1:T(8,128)(2,1)} %dynamic_update_slice.48, bf16[16,2048]{0,1:T(8,128)(2,1)} %copy-done.7, s32[]{:T(128)S(6)} %select_n.184, s32[]{:T(128)} %constant.117.clone.1) | dynamic-update-slice | bytes 131076 | tf_op jit(solution)/shard_map/dynamic_update_slice | solution.py:21
  190.7 6.8 %dynamic_update_slice.50 = bf16[256,2048]{0,1:T(8,128)(2,1)} dynamic-update-slice(bf16[256,2048]{0,1:T(8,128)(2,1)} %dynamic_update_slice.49, bf16[16,2048]{0,1:T(8,128)(2,1)} %copy-done.8, s32[]{:T(128)S(6)} %select_n.186, s32[]{:T(128)} %constant.117.clone.1) | dynamic-update-slice | bytes 131076 | tf_op jit(solution)/shard_map/dynamic_update_slice | solution.py:26
  197.5 6.1 %dynamic_update_slice.51 = bf16[256,2048]{0,1:T(8,128)(2,1)} dynamic-update-slice(bf16[256,2048]{0,1:T(8,128)(2,1)} %dynamic_update_slice.50, bf16[16,2048]{0,1:T(8,128)(2,1)} %collective-permute-done.4, s32[]{:T(128)S(6)} %select_n.188, s32[]{:T(128)} %constant.117.clone.1) | dynamic-update-slice | bytes 131076 | tf_op jit(solution)/shard_map/dynamic_update_slice | solution.py:21
  203.6 6.8 %dynamic_update_slice.52 = bf16[256,2048]{0,1:T(8,128)(2,1)} dynamic-update-slice(bf16[256,2048]{0,1:T(8,128)(2,1)} %dynamic_update_slice.51, bf16[16,2048]{0,1:T(8,128)(2,1)} %collective-permute-done.5, s32[]{:T(128)S(6)} %select_n.190, s32[]{:T(128)} %constant.117.clone.1) | dynamic-update-slice | bytes 131076 | tf_op jit(solution)/shard_map/dynamic_update_slice | solution.py:26
  210.4 6.1 %dynamic_update_slice.53 = bf16[256,2048]{0,1:T(8,128)(2,1)} dynamic-update-slice(bf16[256,2048]{0,1:T(8,128)(2,1)} %dynamic_update_slice.52, bf16[16,2048]{0,1:T(8,128)(2,1)} %collective-permute-done.6, s32[]{:T(128)S(6)} %select_n.192, s32[]{:T(128)} %constant.117.clone.1) | dynamic-update-slice | bytes 131076 | tf_op jit(solution)/shard_map/dynamic_update_slice | solution.py:21
  216.5 6.8 %dynamic_update_slice.54 = bf16[256,2048]{0,1:T(8,128)(2,1)} dynamic-update-slice(bf16[256,2048]{0,1:T(8,128)(2,1)} %dynamic_update_slice.53, bf16[16,2048]{0,1:T(8,128)(2,1)} %collective-permute-done.7, s32[]{:T(128)S(6)} %select_n.194, s32[]{:T(128)} %constant.117.clone.1) | dynamic-update-slice | bytes 131076 | tf_op jit(solution)/shard_map/dynamic_update_slice | solution.py:26
  223.3 6.1 %dynamic_update_slice.55 = bf16[256,2048]{0,1:T(8,128)(2,1)} dynamic-update-slice(bf16[256,2048]{0,1:T(8,128)(2,1)} %dynamic_update_slice.54, bf16[16,2048]{0,1:T(8,128)(2,1)} %collective-permute-done.8, s32[]{:T(128)S(6)} %select_n.196, s32[]{:T(128)} %constant.117.clone.1) | dynamic-update-slice | bytes 131076 | tf_op jit(solution)/shard_map/dynamic_update_slice | solution.py:21
  229.4 6.8 %dynamic_update_slice.56 = bf16[256,2048]{0,1:T(8,128)(2,1)} dynamic-update-slice(bf16[256,2048]{0,1:T(8,128)(2,1)} %dynamic_update_slice.55, bf16[16,2048]{0,1:T(8,128)(2,1)} %collective-permute-done.9, s32[]{:T(128)S(6)} %select_n.198, s32[]{:T(128)} %constant.117.clone.1) | dynamic-update-slice | bytes 131076 | tf_op jit(solution)/shard_map/dynamic_update_slice | solution.py:26
  242.3 6.8 %dynamic_update_slice.58 = bf16[256,2048]{0,1:T(8,128)(2,1)} dynamic-update-slice(bf16[256,2048]{0,1:T(8,128)(2,1)} %dynamic_update_slice.57, bf16[16,2048]{0,1:T(8,128)(2,1)} %collective-permute-done.11, s32[]{:T(128)S(6)} %select_n.202, s32[]{:T(128)} %constant.117.clone.1) | dynamic-update-slice | bytes 131076 | tf_op jit(solution)/shard_map/dynamic_update_slice | solution.py:26
  249.0 6.1 %dynamic_update_slice.59 = bf16[256,2048]{0,1:T(8,128)(2,1)} dynamic-update-slice(bf16[256,2048]{0,1:T(8,128)(2,1)} %dynamic_update_slice.58, bf16[16,2048]{0,1:T(8,128)(2,1)} %collective-permute-done.12, s32[]{:T(128)S(6)} %select_n.204, s32[]{:T(128)} %constant.117.clone.1) | dynamic-update-slice | bytes 131076 | tf_op jit(solution)/shard_map/dynamic_update_slice | solution.py:21
  255.1 6.8 %dynamic_update_slice.60 = bf16[256,2048]{0,1:T(8,128)(2,1)} dynamic-update-slice(bf16[256,2048]{0,1:T(8,128)(2,1)} %dynamic_update_slice.59, bf16[16,2048]{0,1:T(8,128)(2,1)} %collective-permute-done.13, s32[]{:T(128)S(6)} %select_n.206, s32[]{:T(128)} %constant.117.clone.1) | dynamic-update-slice | bytes 131076 | tf_op jit(solution)/shard_map/dynamic_update_slice | solution.py:26
  261.9 6.1 %dynamic_update_slice.61 = bf16[256,2048]{0,1:T(8,128)(2,1)} dynamic-update-slice(bf16[256,2048]{0,1:T(8,128)(2,1)} %dynamic_update_slice.60, bf16[16,2048]{0,1:T(8,128)(2,1)} %collective-permute-done.14, s32[]{:T(128)S(6)} %select_n.208, s32[]{:T(128)} %constant.117.clone.1) | dynamic-update-slice | bytes 131076 | tf_op jit(solution)/shard_map/dynamic_update_slice | solution.py:21
  268.0 6.8 %dynamic_update_slice.62 = bf16[256,2048]{0,1:T(8,128)(2,1)} dynamic-update-slice(bf16[256,2048]{0,1:T(8,128)(2,1)} %dynamic_update_slice.61, bf16[16,2048]{0,1:T(8,128)(2,1)} %collective-permute-done.15, s32[]{:T(128)S(6)} %select_n.210, s32[]{:T(128)} %constant.117.clone.1) | dynamic-update-slice | bytes 131076 | tf_op jit(solution)/shard_map/dynamic_update_slice | solution.py:26
  285.0 60.0 %pmax.7 = f32[256,16]{0,1:T(8,128)S(1)} all-reduce(f32[256,16]{0,1:T(8,128)S(1)} %get-tuple-element.35), channel_id=1, replica_groups=mesh['groups'=2,'rows'=16] {'rows'}, use_global_device_ids=true, to_apply=%region_9.10 | all-reduce | flops 4096 | bytes 32768 | tf_op jit(solution)/shard_map/pmax | solution.py:164
  353.6 58.8 %psum.15 = f32[256,16]{0,1:T(8,128)S(1)} all-reduce(f32[256,16]{0,1:T(8,128)S(1)} %get-tuple-element.5), channel_id=1, replica_groups=mesh['groups'=2,'rows'=16] {'rows'}, use_global_device_ids=true, to_apply=%region_13.14 | all-reduce | flops 4096 | bytes 32768 | tf_op jit(solution)/shard_map/psum | solution.py:168
  412.3 7.6 %pad_maximum_fusion = bf16[2,1152,2048]{2,1,0:T(8,128)(2,1)} fusion(bf16[2,384,2048]{2,1,0:T(8,128)(2,1)} %collective-permute-done.1, bf16[2,384,2048]{2,1,0:T(8,128)(2,1)} %param.9, bf16[2,384,2048]{2,1,0:T(8,128)(2,1)} %collective-permute-done), kind=kLoop, calls=%fused_computation | loop fusion | flops 28311552 | bytes 18874368 | tf_op jit(solution)/shard_map/concatenate | solution.py:38
  420.0 11.1 %copy.104 = bf16[288,8,16,128]{3,2,1,0:T(8,128)(2,1)} copy(bf16[288,8,16,128]{3,1,2,0:T(8,128)(2,1)} %bitcast.284) | data formatting | bytes 18874368
  462.4 6.8 %fusion.135 = (bf16[1,256,2048]{2,0,1:T(2,128)(2,1)}, bf16[1,256,2048]{2,0,1:T(2,128)(2,1)}) fusion(bf16[2,256,2048]{2,0,1:T(2,128)(2,1)} %all-gather.2.cloned.1.call-done), kind=kLoop, calls=%fused_computation.156 | loop fusion | bytes 4194304 | tf_op jit(solution)/shard_map/slice | solution.py:122
  (111 shorter events, 153.6 us)
Async XLA Ops:
  7.2 130.7 %copy-start = (bf16[384,2048]{1,0:T(8,128)(2,1)S(1)}, bf16[384,2048]{1,0:T(8,128)(2,1)}, u32[]{:S(2)}) copy-start(bf16[384,2048]{1,0:T(8,128)(2,1)} %param.8) | copy-start | bytes 4718596
  7.2 455.2 %all-gather.2.cloned.1.call-start = ((), (), s32[]{:S(2)}) async-start(), calls=%async_computation | async-start | bytes 2228224 | tf_op jit(solution)/shard_map/all_gather | solution.py:119
  8.5 31.8 %copy-start.3 = (bf16[16,2048]{0,1:T(8,128)(2,1)}, bf16[16,2048]{0,1:T(8,128)(2,1)S(1)}, u32[]{:S(2)}) copy-start(bf16[16,2048]{0,1:T(8,128)(2,1)S(1)} %copy.74) | copy-start | bytes 196612
  8.5 12.5 %collective-permute-start.2 = (bf16[16,2048]{0,1:T(8,128)(2,1)S(1)}, bf16[16,2048]{0,1:T(8,128)(2,1)S(1)}, u32[]{:S(2)}, u32[]{:S(2)}) collective-permute-start(bf16[16,2048]{0,1:T(8,128)(2,1)S(1)} %copy.74), channel_id=1, source_target_pairs={{0,1},{1,2},{2,3},{3,4},{4,5},{5,6},{6,7},{7,8},{8,9},{9,10},{10,1... | collective-permute-start | bytes 196616 | tf_op jit(solution)/shard_map/ppermute | solution.py:20
  9.0 23.5 %collective-permute-start.3 = (bf16[16,2048]{0,1:T(8,128)(2,1)S(1)}, bf16[16,2048]{0,1:T(8,128)(2,1)S(1)}, u32[]{:S(2)}, u32[]{:S(2)}) collective-permute-start(bf16[16,2048]{0,1:T(8,128)(2,1)S(1)} %copy.74), channel_id=1, source_target_pairs={{0,15},{1,0},{2,1},{3,2},{4,3},{5,4},{6,5},{7,6},{8,7},{9,8},{10,9... | collective-permute-start | bytes 196616 | tf_op jit(solution)/shard_map/ppermute | solution.py:25
  20.9 19.3 %copy-start.7 = (bf16[16,2048]{0,1:T(8,128)(2,1)}, bf16[16,2048]{0,1:T(8,128)(2,1)S(1)}, u32[]{:S(2)}) copy-start(bf16[16,2048]{0,1:T(8,128)(2,1)S(1)} %collective-permute-done.2) | copy-start | bytes 196612
  20.9 15.3 %collective-permute-start.4 = (bf16[16,2048]{0,1:T(8,128)(2,1)S(1)}, bf16[16,2048]{0,1:T(8,128)(2,1)}, u32[]{:S(2)}, u32[]{:S(2)}) collective-permute-start(bf16[16,2048]{0,1:T(8,128)(2,1)S(1)} %collective-permute-done.2), channel_id=1, source_target_pairs={{0,1},{1,2},{2,3},{3,4},{4,5},{5,6},{6,7},{7,8},{8,9},{9,10},{10,1... | collective-permute-start | bytes 196616 | tf_op jit(solution)/shard_map/ppermute | solution.py:20
  23.3 389.0 %collective-permute-start = (bf16[2,384,2048]{2,1,0:T(8,128)(2,1)}, bf16[2,384,2048]{2,1,0:T(8,128)(2,1)}, u32[]{:S(2)}, u32[]{:S(2)}) collective-permute-start(bf16[2,384,2048]{2,1,0:T(8,128)(2,1)} %param.9), channel_id=1, source_target_pairs={{0,1},{1,2},{2,3},{3,4},{4,5},{5,6},{6,7},{7,8},{8,9},{9,10},{10,1... | collective-permute-start | bytes 9437192 | tf_op jit(solution)/shard_map/ppermute | solution.py:40
  29.4 383.0 %collective-permute-start.1 = (bf16[2,384,2048]{2,1,0:T(8,128)(2,1)}, bf16[2,384,2048]{2,1,0:T(8,128)(2,1)}, u32[]{:S(2)}, u32[]{:S(2)}) collective-permute-start(bf16[2,384,2048]{2,1,0:T(8,128)(2,1)} %param.9), channel_id=1, source_target_pairs={{1,0},{2,1},{3,2},{4,3},{5,4},{6,5},{7,6},{8,7},{9,8},{10,9},{11,1... | collective-permute-start | bytes 9437192 | tf_op jit(solution)/shard_map/ppermute | solution.py:42
  32.4 91.0 %copy-start.10 = (s32[16,2]{0,1:T(2,128)S(1)}, s32[16,2]{0,1:T(2,128)}, u32[]{:S(2)}) copy-start(s32[16,2]{0,1:T(2,128)} %param.13) | copy-start | bytes 388
  32.4 460.2 %all-reduce.2.cloned.1.call-start = ((), (), s32[]{:S(2)}) async-start(), calls=%async_computation.1 | async-start | bytes 4194304 | tf_op jit(solution)/shard_map/psum | solution.py:168
  32.5 11.9 %collective-permute-start.5 = (bf16[16,2048]{0,1:T(8,128)(2,1)S(1)}, bf16[16,2048]{0,1:T(8,128)(2,1)}, u32[]{:S(2)}, u32[]{:S(2)}) collective-permute-start(bf16[16,2048]{0,1:T(8,128)(2,1)S(1)} %collective-permute-done.3), channel_id=1, source_target_pairs={{0,15},{1,0},{2,1},{3,2},{4,3},{5,4},{6,5},{7,6},{8,7},{9,8},{10,9... | collective-permute-start | bytes 196616 | tf_op jit(solution)/shard_map/ppermute | solution.py:25
  36.2 28.6 %collective-permute-start.6 = (bf16[16,2048]{0,1:T(8,128)(2,1)}, bf16[16,2048]{0,1:T(8,128)(2,1)}, u32[]{:S(2)}, u32[]{:S(2)}) collective-permute-start(bf16[16,2048]{0,1:T(8,128)(2,1)} %collective-permute-done.4), channel_id=1, source_target_pairs={{0,1},{1,2},{2,3},{3,4},{4,5},{5,6},{6,7},{7,8},{8,9},{9,10},{10,1... | collective-permute-start | bytes 196616 | tf_op jit(solution)/shard_map/ppermute | solution.py:20
  44.3 80.9 %collective-permute-start.7 = (bf16[16,2048]{0,1:T(8,128)(2,1)}, bf16[16,2048]{0,1:T(8,128)(2,1)}, u32[]{:S(2)}, u32[]{:S(2)}) collective-permute-start(bf16[16,2048]{0,1:T(8,128)(2,1)} %collective-permute-done.5), channel_id=1, source_target_pairs={{0,15},{1,0},{2,1},{3,2},{4,3},{5,4},{6,5},{7,6},{8,7},{9,8},{10,9... | collective-permute-start | bytes 196616 | tf_op jit(solution)/shard_map/ppermute | solution.py:25
  64.8 61.5 %collective-permute-start.8 = (bf16[16,2048]{0,1:T(8,128)(2,1)}, bf16[16,2048]{0,1:T(8,128)(2,1)}, u32[]{:S(2)}, u32[]{:S(2)}) collective-permute-start(bf16[16,2048]{0,1:T(8,128)(2,1)} %collective-permute-done.6), channel_id=1, source_target_pairs={{0,1},{1,2},{2,3},{3,4},{4,5},{5,6},{6,7},{7,8},{8,9},{9,10},{10,1... | collective-permute-start | bytes 196616 | tf_op jit(solution)/shard_map/ppermute | solution.py:20
  125.2 21.2 %collective-permute-start.9 = (bf16[16,2048]{0,1:T(8,128)(2,1)}, bf16[16,2048]{0,1:T(8,128)(2,1)}, u32[]{:S(2)}, u32[]{:S(2)}) collective-permute-start(bf16[16,2048]{0,1:T(8,128)(2,1)} %collective-permute-done.7), channel_id=1, source_target_pairs={{0,15},{1,0},{2,1},{3,2},{4,3},{5,4},{6,5},{7,6},{8,7},{9,8},{10,9... | collective-permute-start | bytes 196616 | tf_op jit(solution)/shard_map/ppermute | solution.py:25
  126.3 20.2 %collective-permute-start.10 = (bf16[16,2048]{0,1:T(8,128)(2,1)}, bf16[16,2048]{0,1:T(8,128)(2,1)}, u32[]{:S(2)}, u32[]{:S(2)}) collective-permute-start(bf16[16,2048]{0,1:T(8,128)(2,1)} %collective-permute-done.8), channel_id=1, source_target_pairs={{0,1},{1,2},{2,3},{3,4},{4,5},{5,6},{6,7},{7,8},{8,9},{9,10},{10,1... | collective-permute-start | bytes 196616 | tf_op jit(solution)/shard_map/ppermute | solution.py:20
  146.5 10.9 %collective-permute-start.11 = (bf16[16,2048]{0,1:T(8,128)(2,1)}, bf16[16,2048]{0,1:T(8,128)(2,1)}, u32[]{:S(2)}, u32[]{:S(2)}) collective-permute-start(bf16[16,2048]{0,1:T(8,128)(2,1)} %collective-permute-done.9), channel_id=1, source_target_pairs={{0,15},{1,0},{2,1},{3,2},{4,3},{5,4},{6,5},{7,6},{8,7},{9,8},{10,9... | collective-permute-start | bytes 196616 | tf_op jit(solution)/shard_map/ppermute | solution.py:25
  146.5 12.9 %collective-permute-start.12 = (bf16[16,2048]{0,1:T(8,128)(2,1)}, bf16[16,2048]{0,1:T(8,128)(2,1)}, u32[]{:S(2)}, u32[]{:S(2)}) collective-permute-start(bf16[16,2048]{0,1:T(8,128)(2,1)} %collective-permute-done.10), channel_id=1, source_target_pairs={{0,1},{1,2},{2,3},{3,4},{4,5},{5,6},{6,7},{7,8},{8,9},{9,10},{10,1... | collective-permute-start | bytes 196616 | tf_op jit(solution)/shard_map/ppermute | solution.py:20
  149.0 28.6 %copy-start.11 = (s32[256]{0:T(256)S(1)}, s32[256]{0:T(256)}, u32[]{:S(2)}) copy-start(s32[256]{0:T(256)} %param.12) | copy-start | bytes 3076
  157.4 9.0 %collective-permute-start.13 = (bf16[16,2048]{0,1:T(8,128)(2,1)}, bf16[16,2048]{0,1:T(8,128)(2,1)}, u32[]{:S(2)}, u32[]{:S(2)}) collective-permute-start(bf16[16,2048]{0,1:T(8,128)(2,1)} %collective-permute-done.11), channel_id=1, source_target_pairs={{0,15},{1,0},{2,1},{3,2},{4,3},{5,4},{6,5},{7,6},{8,7},{9,8},{10,9... | collective-permute-start | bytes 196616 | tf_op jit(solution)/shard_map/ppermute | solution.py:25
  159.4 11.7 %collective-permute-start.14 = (bf16[16,2048]{0,1:T(8,128)(2,1)}, bf16[16,2048]{0,1:T(8,128)(2,1)}, u32[]{:S(2)}, u32[]{:S(2)}) collective-permute-start(bf16[16,2048]{0,1:T(8,128)(2,1)} %collective-permute-done.12), channel_id=1, source_target_pairs={{0,1},{1,2},{2,3},{3,4},{4,5},{5,6},{6,7},{7,8},{8,9},{9,10},{10,1... | collective-permute-start | bytes 196616 | tf_op jit(solution)/shard_map/ppermute | solution.py:20
  166.5 101.6 %collective-permute-start.15 = (bf16[16,2048]{0,1:T(8,128)(2,1)}, bf16[16,2048]{0,1:T(8,128)(2,1)}, u32[]{:S(2)}, u32[]{:S(2)}) collective-permute-start(bf16[16,2048]{0,1:T(8,128)(2,1)} %collective-permute-done.13), channel_id=1, source_target_pairs={{0,15},{1,0},{2,1},{3,2},{4,3},{5,4},{6,5},{7,6},{8,7},{9,8},{10,9... | collective-permute-start | bytes 196616 | tf_op jit(solution)/shard_map/ppermute | solution.py:25
  171.2 103.6 %collective-permute-start.16 = (bf16[16,2048]{0,1:T(8,128)(2,1)}, bf16[16,2048]{0,1:T(8,128)(2,1)}, u32[]{:S(2)}, u32[]{:S(2)}) collective-permute-start(bf16[16,2048]{0,1:T(8,128)(2,1)} %collective-permute-done.14), channel_id=1, source_target_pairs={{0,1},{1,2},{2,3},{3,4},{4,5},{5,6},{6,7},{7,8},{8,9},{9,10},{10,1... | collective-permute-start | bytes 196616 | tf_op jit(solution)/shard_map/ppermute | solution.py:20
  (13 other events, 49.7 us)
Sparse Core Ops, SparseCore 0:
  32.5 57.2 all-gather.1
  353.7 95.2 all-reduce.1
